TPU v7x, 32 devices: a whole 2x2x4 slice. The times are simulated.
32 devices in a mesh: sy: 4 (over z), sx: 8 (over y, x, core).
Axes of the slice: x: 2, y: 2, z: 4, core: 2. Of those that a mesh axis runs over, the one named last changes fastest.
Arguments:
- sky_image: float32 [1024, 1024], P('sy', 'sx'), may hold values from -6 to 6
- observed: float32 [1024, 1024], P('sy', 'sx'), may hold values from -6 to 6
- noise_weight: float32 [1024, 1024], P('sy', 'sx'), may hold values from 0.25 to 4
- basis_tiles: bfloat16 [128, 128, 128], P(('sy', 'sx')), may hold values from -3 to 3
- intersection: int32 [8, 8, 4], replicated, may hold values from 0 to 127, as said below
- counts: int32 [8, 8], P('sy', 'sx'), may hold values from 1 to 4
- transfer: float32 [4, 2, 1024, 1024], P(None, None, ('sy', 'sx')), may hold values from -6 to 6
Outputs:
- residual: float32 [1024, 1024], P('sy', 'sx')
- gradient: float32 [1024, 1024], P('sy', 'sx')
Inputs may be any that keep to these rules, and one draw needn't show every extreme that they name: `intersection`: every entry names a basis tile held by a device with the same sy index as the sky tile. Of the 8 entries of one device's sky tiles, at most 2 name tiles held by any one device, and in every draw each device reaches 2 at one holder.
All inputs are finite; a program needn't handle non-finite values.
Results may differ from a plain program's by a relative error of at most 0.00045.
Values may be sent and summed in bfloat16 or wider, within the bound.
A program may use at most 128 MiB of HBM per device.

v0:
```python
import jax
import jax.numpy as jnp
import numpy as np
from jax import lax
from jax.experimental import pallas as pl
from jax.experimental.pallas import tpu as pltpu
from jax.sharding import PartitionSpec as P

radix = 128
highest = lax.Precision.HIGHEST
tv_weight = 0.5
smoothing = 0.25


def with_halo(block, sides, width):
    for axis, dim in sides:
        count = lax.axis_size(axis)
        forward = [(i, i + 1) for i in range(count - 1)]
        forward.append((count - 1, 0))
        backward = [(target, source) for source, target in forward]
        low = lax.ppermute(
            lax.slice_in_dim(block, block.shape[dim] - width, None, axis=dim), axis, forward
        )
        high = lax.ppermute(lax.slice_in_dim(block, 0, width, axis=dim), axis, backward)
        block = jnp.concatenate([low, block, high], axis=dim)
    return block


def circle(left_index, right_index, length, orient):
    product = left_index[:, None] * right_index[None, :] % length
    angles = product.astype(jnp.float32) * (2.0 * jnp.pi / length)
    return (jnp.cos(angles), orient * jnp.sin(angles))


def contract(pattern, operand, matrix):
    return jnp.einsum(pattern, operand, matrix, precision=highest)


def forward_last(stacked):
    num_parts, num_fields, num_lines, length = stacked.shape
    short_size = length // radix
    pieces = stacked.reshape(num_parts, num_fields, num_lines, short_size, radix)
    short_index = jnp.arange(short_size, dtype=jnp.int32)
    long_index = jnp.arange(radix, dtype=jnp.int32)
    cos_short, sin_short = circle(short_index, short_index, short_size, -1.0)
    cos_turn, sin_turn = circle(short_index, long_index, length, -1.0)
    cos_long, sin_long = circle(long_index, long_index, radix, -1.0)
    first_form = "fmba,bk->fmka"
    real_part = contract(first_form, pieces[0], cos_short)
    imag_part = contract(first_form, pieces[0], sin_short)
    if num_parts == 2:
        real_part = real_part - contract(first_form, pieces[1], sin_short)
        imag_part = imag_part + contract(first_form, pieces[1], cos_short)
    turned_real = real_part * cos_turn - imag_part * sin_turn
    turned_imag = real_part * sin_turn + imag_part * cos_turn
    second_form = "fmka,aj->fmkj"
    out_real = contract(second_form, turned_real, cos_long) - contract(
        second_form, turned_imag, sin_long
    )
    out_imag = contract(second_form, turned_real, sin_long) + contract(
        second_form, turned_imag, cos_long
    )
    return jnp.stack([out_real, out_imag]).reshape(2, num_fields, num_lines, length)


def inverse_last(stacked, real_only):
    num_fields, num_lines, length = (stacked.shape[1], stacked.shape[2], stacked.shape[3])
    short_size = length // radix
    pieces = stacked.reshape(2, num_fields, num_lines, short_size, radix)
    short_index = jnp.arange(short_size, dtype=jnp.int32)
    long_index = jnp.arange(radix, dtype=jnp.int32)
    cos_long, sin_long = circle(long_index, long_index, radix, 1.0)
    cos_turn, sin_turn = circle(short_index, long_index, length, 1.0)
    cos_short, sin_short = circle(short_index, short_index, short_size, 1.0)
    first_form = "fmkj,ja->fmka"
    real_part = contract(first_form, pieces[0], cos_long) - contract(
        first_form, pieces[1], sin_long
    )
    imag_part = contract(first_form, pieces[0], sin_long) + contract(
        first_form, pieces[1], cos_long
    )
    turned_real = real_part * cos_turn - imag_part * sin_turn
    turned_imag = real_part * sin_turn + imag_part * cos_turn
    second_form = "fmka,kb->fmba"
    out_real = contract(second_form, turned_real, cos_short) - contract(
        second_form, turned_imag, sin_short
    )
    if real_only:
        return out_real.reshape(1, num_fields, num_lines, length)
    out_imag = contract(second_form, turned_real, sin_short) + contract(
        second_form, turned_imag, cos_short
    )
    return jnp.stack([out_real, out_imag]).reshape(2, num_fields, num_lines, length)


def to_spectra(pixels):
    columns = lax.all_to_all(
        jnp.swapaxes(pixels, 2, 3), "sy", split_axis=2, concat_axis=3, tiled=True
    )
    along_y = forward_last(columns)
    blocks = lax.all_to_all(along_y, "sy", split_axis=3, concat_axis=2, tiled=True)
    lines = lax.all_to_all(
        jnp.swapaxes(blocks, 2, 3), "sx", split_axis=2, concat_axis=3, tiled=True
    )
    return forward_last(lines)


def from_spectra(spectrum, normalizer):
    along_x = inverse_last(spectrum, False)
    blocks = lax.all_to_all(along_x, "sx", split_axis=3, concat_axis=2, tiled=True)
    columns = lax.all_to_all(
        jnp.swapaxes(blocks, 2, 3), "sy", split_axis=2, concat_axis=3, tiled=True
    )
    values = inverse_last(columns, True) * normalizer
    pixel_blocks = lax.all_to_all(values, "sy", split_axis=3, concat_axis=2, tiled=True)
    return jnp.swapaxes(pixel_blocks, 2, 3)[0]


def generic_device(sky_image, observed, noise_weight, basis_tiles, intersection, counts, transfer):
    height, breadth = sky_image.shape
    pool_size, tile_side = (basis_tiles.shape[0], basis_tiles.shape[1])
    components = intersection.shape[2]
    tiles_down = height // tile_side
    tiles_across = breadth // tile_side
    band_size = lax.axis_size("sx")
    sky_row = lax.axis_index("sy")
    sky_column = lax.axis_index("sx")
    num_requests = tiles_down * tiles_across * components
    zero_index = jnp.zeros((), jnp.int32)
    own_lists = lax.dynamic_slice(
        intersection,
        (sky_row * tiles_down, sky_column * tiles_across, zero_index),
        (tiles_down, tiles_across, components),
    ).reshape(num_requests)
    band_start = sky_row * band_size * pool_size
    band_index = own_lists - band_start
    flat_tiles = basis_tiles.reshape(pool_size, tile_side * tile_side)
    piece = lax.all_gather(flat_tiles, "sx", axis=0, tiled=True)
    piece_count = piece.shape[0]
    hits = (band_index[:, None] == jnp.arange(piece_count, dtype=jnp.int32)[None, :]).astype(
        jnp.bfloat16
    )
    coefficient = jnp.dot(hits, piece, preferred_element_type=jnp.float32)
    in_use = (jnp.arange(components, dtype=jnp.int32)[None, None, :] < counts[:, :, None]).astype(
        jnp.float32
    )
    coef_maps = (
        coefficient.reshape(tiles_down, tiles_across, components, tile_side, tile_side)
        * in_use[:, :, :, None, None]
    )
    weights = coef_maps.transpose(2, 0, 3, 1, 4).reshape(components, height, breadth)
    normalizer = 1.0 / (transfer.shape[2] * lax.axis_size("sy") * band_size * transfer.shape[3])
    spectra = to_spectra((weights * sky_image[None])[None])
    trans_real = transfer[:, 0]
    trans_imag = transfer[:, 1]
    model_real = jnp.sum(spectra[0] * trans_real - spectra[1] * trans_imag, axis=0)
    model_imag = jnp.sum(spectra[0] * trans_imag + spectra[1] * trans_real, axis=0)
    blurred = from_spectra(jnp.stack([model_real, model_imag])[:, None], normalizer)[0]
    residual = noise_weight * (blurred - observed)
    back_spectrum = to_spectra(residual[None, None])
    pull_real = back_spectrum[0] * trans_real + back_spectrum[1] * trans_imag
    pull_imag = back_spectrum[1] * trans_real - back_spectrum[0] * trans_imag
    pulled = from_spectra(jnp.stack([pull_real, pull_imag]), normalizer)
    data_grad = jnp.sum(weights * pulled, axis=0)
    framed = with_halo(sky_image, (("sy", 0), ("sx", 1)), 1)
    step_x = framed[:-1, 1:] - framed[:-1, :-1]
    step_y = framed[1:, :-1] - framed[:-1, :-1]
    magnitude = jnp.sqrt(step_x * step_x + step_y * step_y + smoothing)
    flow_x = step_x / magnitude
    flow_y = step_y / magnitude
    spread = flow_x[1:, 1:] - flow_x[1:, :-1] + flow_y[1:, 1:] - flow_y[:-1, 1:]
    gradient = data_grad - tv_weight * spread
    return (residual, gradient)


lanes = 128
group = 32
num_groups = 4
bands = 4
band_size = 8
devices = 32
size = 1024
MESH = pl.DeviceIdType.MESH


def split_table(values):
    high = values.astype(jnp.bfloat16)
    return high, (values - high.astype(np.float64)).astype(jnp.bfloat16)


def tables():
    spot = np.arange(size)
    owner, column = (spot // group, spot % group)
    pixel = (owner % band_size) * lanes + (owner // band_size) * group + column
    frequency = (size // radix) * (spot % radix) + spot // radix
    angle = (frequency[:, None] * spot[None, :] % size) * (2.0 * np.pi / size)
    parts = np.stack([np.cos(angle), -np.sin(angle)]).reshape(2, devices, group, size)
    along_y = parts.transpose(1, 0, 2, 3).reshape(2 * size, size)
    angle = (pixel[:, None] * frequency[None, :] % size) * (2.0 * np.pi / size)
    cos_high, cos_low = split_table(np.cos(angle))
    sin_high, sin_low = split_table(np.sin(angle))
    return (
        *split_table(along_y),
        cos_high,
        sin_high,
        cos_low,
        sin_low,
        *split_table(np.ascontiguousarray(along_y.T)),
    )


def split(values):
    high = values.astype(jnp.bfloat16)
    return high, (values - high.astype(jnp.float32)).astype(jnp.bfloat16)


def mul(left, right):
    return jnp.dot(left, right, preferred_element_type=jnp.float32)


def mul_t(left, right):
    return lax.dot_general(
        left, right, (((1,), (1,)), ((), ())), preferred_element_type=jnp.float32
    )


def cut(values, index):
    return values[:, index * group : (index + 1) * group]


def lane_groups(rows):
    return lax.broadcasted_iota(jnp.int32, (rows, lanes), 1) // group


def pick_groups(pieces):
    where = lane_groups(pieces[0].shape[0])
    out = pieces[0]
    for index in range(1, num_groups):
        out = jnp.where(where == index, pieces[index], out)
    return out


def fold(values):
    values = values + pltpu.roll(values, 64, 1)
    return values + pltpu.roll(values, 32, 1)


def pull(total, sky, left, right, below, above, below_left, above_right):
    rows = sky.shape[0]
    lane = lax.broadcasted_iota(jnp.int32, sky.shape, 1)
    row = lax.broadcasted_iota(jnp.int32, sky.shape, 0)

    def flows(step_x, step_y):
        magnitude = jnp.sqrt(step_x * step_x + step_y * step_y + smoothing)
        return step_x / magnitude, step_y / magnitude

    next_x = jnp.where(lane == lanes - 1, right, pltpu.roll(sky, lanes - 1, 1))
    next_y = jnp.where(row == rows - 1, below, pltpu.roll(sky, rows - 1, 0))
    flow_x, flow_y = flows(next_x - sky, next_y - sky)
    left_next = jnp.where(row == rows - 1, below_left, pltpu.roll(left, rows - 1, 0))
    side_x, _ = flows(sky - left, left_next - left)
    side_x = side_x[:, 0:1]
    above_next = jnp.where(lane[0:8] == lanes - 1, above_right, pltpu.roll(above, lanes - 1, 1))
    _, top_y = flows(above_next - above, sky[0:1] - above)
    before_x = jnp.where(lane == 0, side_x, pltpu.roll(flow_x, 1, 1))
    before_y = jnp.where(row == 0, top_y[7:8], pltpu.roll(flow_y, 1, 0))
    total[...] = flow_x - before_x + flow_y - before_y


def kernel(
    sky, seen, noise, mask, basis, tile_mult, pick_mult,
    trans_hbm, fyh_hbm, fyl_hbm, cxh_hbm, sxh_hbm, cxl_hbm, sxl_hbm, gh_hbm, gl_hbm,
    res_out, grad_out,
    trans, fyh, fyl, cxh, sxh, cxl, sxl, gh, gl,
    sky_s, sky_r, seen_s, seen_r, noise_s, noise_r, tile_s, tile_r,
    two_s, two_r, three_s, three_r, four_s, four_r, five_s, five_r,
    res_s, res_r, grad_s, grad_r,
    halo_left, halo_right, halo_below, halo_above, halo_bl, halo_ar,
    weights, fields, wide, narrow, tall, spread,
    load_sem, send_sem, recv_sem,
):
    my_y, my_x = (lax.axis_index("sy"), lax.axis_index("sx"))
    me = my_y * band_size + my_x
    barrier = pltpu.get_barrier_semaphore()

    def greet(step, carry):
        other = lax.rem(me + step, devices)
        pl.semaphore_signal(
            barrier, inc=1, device_id=(other // band_size, lax.rem(other, band_size)),
            device_id_type=MESH,
        )
        return carry

    lax.fori_loop(1, devices, greet, 0)
    loads = []
    pairs = (
        (fyh_hbm, fyh), (fyl_hbm, fyl), (cxh_hbm, cxh), (sxh_hbm, sxh), (cxl_hbm, cxl),
        (sxl_hbm, sxl), (trans_hbm, trans), (gh_hbm, gh), (gl_hbm, gl),
    )
    for index, (source, target) in enumerate(pairs):
        loads.append(pltpu.make_async_copy(source, target, load_sem.at[index]))
        loads[-1].start()

    def send(source, target, phase, where):
        pltpu.make_async_remote_copy(
            src_ref=source, dst_ref=target, send_sem=send_sem.at[phase],
            recv_sem=recv_sem.at[phase], device_id=where, device_id_type=MESH,
        ).start()

    def total_of(buffer, phase):
        part = buffer.at[pl.ds(0, buffer.shape[0] - 1)]
        return pltpu.make_async_remote_copy(
            src_ref=part, dst_ref=part, send_sem=send_sem.at[phase],
            recv_sem=recv_sem.at[phase], device_id=(lax.rem(my_y + 1, bands), my_x),
            device_id_type=MESH,
        )

    def to_all(source, target, phase, other):
        @pl.when(other != me)
        def _():
            send(
                source.at[other], target.at[me], phase,
                (other // band_size, lax.rem(other, band_size)),
            )

        @pl.when(other == me)
        def _():
            target[me] = source[me]

    def to_band(source, target, phase, other):
        @pl.when(other != my_y)
        def _():
            send(source.at[other], target.at[my_y], phase, (other, my_x))

        @pl.when(other == my_y)
        def _():
            target[my_y] = source[my_y]

    def pack(block, other):
        return jnp.concatenate(
            [cut(block[g * 64 : (g + 1) * 64], other) for g in range(num_groups)], axis=1
        )

    for other in range(bands):
        sky_s[other, 0:64] = pack(sky[...], other)
        sky_s[other, 64:72] = mask[...]
    pl.semaphore_wait(barrier, devices - 1)
    for other in range(bands):
        to_band(sky_s, sky_r, 0, other)

    for other in range(bands):
        packs = []
        for t in range(4):
            part = cut(basis[t].astype(jnp.float32), other)
            packs.append(
                jnp.concatenate([part[0:64], part[0:64], part[64:128], part[64:128]], axis=1)
            )

        def choose(column, carry):
            acc = tile_mult[column, 0:1] * packs[0]
            for t in range(1, 4):
                acc = acc + tile_mult[column, t : t + 1] * packs[t]
            tile_s[other * band_size + column] = acc.astype(jnp.bfloat16)
            to_all(tile_s, tile_r, 1, other * band_size + column)
            return carry

        lax.fori_loop(0, band_size, choose, 0)

    for other in range(bands):
        seen_s[other] = pack(seen[...], other)
        noise_s[other] = pack(noise[...], other)
        to_band(seen_s, seen_r, 2, other)
        to_band(noise_s, noise_r, 3, other)
    up, down = (lax.rem(my_y + bands - 1, bands), lax.rem(my_y + 1, bands))
    west, east = (lax.rem(my_x + band_size - 1, band_size), lax.rem(my_x + 1, band_size))
    first, last = (sky.at[pl.ds(0, 8)], sky.at[pl.ds(248, 8)])
    halos = (
        (sky_s.at[0, pl.ds(0, 64)], halo_right, (my_y, west)),
        (sky_s.at[bands - 1, pl.ds(0, 64)], halo_left, (my_y, east)),
        (first, halo_below, (up, my_x)),
        (first, halo_bl, (up, east)),
        (last, halo_above, (down, my_x)),
        (last, halo_ar, (down, west)),
    )
    for index, (source, target, where) in enumerate(halos):
        send(source, target, 9 + index, where)

    total_of(sky_r, 0).wait_recv()
    total_of(tile_r, 1).wait_recv()

    def weigh(band, carry):
        parts = []
        for e in range(8):
            acc = None
            for h in range(band_size):
                term = pick_mult[band * 8 + e, h : h + 1] * tile_r[band * band_size + h].astype(
                    jnp.float32
                )
                acc = term if acc is None else acc + term
            acc = (acc + pltpu.roll(acc, 96, 1)) * sky_r[band, 64 + e : 65 + e]
            parts.append(acc)
        for g in range(num_groups):
            down_tile, half = (g // 2, g % 2)
            block = jnp.concatenate(
                [cut(parts[down_tile * 4 + k], 2 * half) for k in range(4)], axis=1
            )
            rows = pl.ds(pl.multiple_of(band * 256 + g * 64, 64), 64)
            weights[rows] = block
            high, low = split(
                block * jnp.concatenate([cut(sky_r[band, 0:64], g)] * num_groups, axis=1)
            )
            fields[rows, 0:128] = high
            fields[rows, 128:256] = low
        return carry

    lax.fori_loop(0, bands, weigh, 0)
    loads[0].wait()
    loads[1].wait()

    def along_y(step):
        part = lax.rem(me // 4 + 1 + step, 8)
        rows = pl.ds(pl.multiple_of(part * 256, 256), 256)
        both = mul(fyh[rows], fields[...])
        return part, both[:, 0:128] + both[:, 128:256] + mul(fyl[rows], fields[:, 0:128])

    def forward_y(step, carry):
        part, out = along_y(step)
        for j in range(4):
            other = part * 4 + j
            two_s[other] = out[j * 64 : (j + 1) * 64]
            to_all(two_s, two_r, 4, other)
        return carry

    lax.fori_loop(0, 8, forward_y, 0)

    for index, (source, target, where) in enumerate(halos):
        pltpu.make_async_remote_copy(
            src_ref=source, dst_ref=target, send_sem=send_sem.at[9 + index],
            recv_sem=recv_sem.at[9 + index], device_id=where, device_id_type=MESH,
        ).wait()

    def side(buffer, lane):
        return jnp.concatenate(
            [
                buffer[:, g * group + lane : g * group + lane + 1] + jnp.zeros((64, lanes))
                for g in range(num_groups)
            ],
            axis=0,
        )

    pull(
        spread, sky[...], side(halo_left, group - 1), side(halo_right, 0), halo_below[0:1],
        halo_above[...], halo_bl[0:1, 127:128], halo_ar[7:8, 0:1],
    )

    for index in range(2, 7):
        loads[index].wait()
    total_of(two_r, 4).wait_recv()

    def gather_two(g, carry):
        at = pl.ds(pl.multiple_of(g * 128, 128), 128)
        for c in range(2):
            blocks = [two_r[4 * g + j, c * 32 : (c + 1) * 32] for j in range(4)]
            for k in range(4):
                high, low = split(jnp.concatenate([cut(block, k) for block in blocks], axis=1))
                row = c * 128 + k * 32
                wide[row : row + 32, at] = high
                wide[256 + row : 288 + row, at] = low
        return carry

    lax.fori_loop(0, 8, gather_two, 0)

    def along_x(buffer, half, at):
        cos_part = mul(buffer[...], cxh[:, at])
        sin_part = mul(buffer[...], sxh[:, at])
        cos_part = cos_part[0:half] + cos_part[half:] + mul(buffer[0:half], cxl[:, at])
        sin_part = sin_part[0:half] + sin_part[half:] + mul(buffer[0:half], sxl[:, at])
        q = half // 2
        return cos_part[0:q] + sin_part[q:half], cos_part[q:half] - sin_part[0:q]

    def back_x(buffer, half, rows):
        cos_part = mul_t(buffer[...], cxh[rows])
        sin_part = mul_t(buffer[...], sxh[rows])
        cos_part = cos_part[0:half] + cos_part[half:] + mul_t(buffer[0:half], cxl[rows])
        sin_part = sin_part[0:half] + sin_part[half:] + mul_t(buffer[0:half], sxl[rows])
        q = half // 2
        return cos_part[0:q] - sin_part[q:half], cos_part[q:half] + sin_part[0:q]

    def model(step, carry):
        at = pl.ds(pl.multiple_of(step * 256, 256), 256)
        real, imag = along_x(wide, 256, at)
        sum_real, sum_imag = (0.0, 0.0)
        for k in range(4):
            rows = slice(k * 32, (k + 1) * 32)
            trans_real, trans_imag = (trans[k, 0, :, at], trans[k, 1, :, at])
            sum_real = sum_real + real[rows] * trans_real - imag[rows] * trans_imag
            sum_imag = sum_imag + real[rows] * trans_imag + imag[rows] * trans_real
        for c, part in enumerate((sum_real, sum_imag)):
            high, low = split(part)
            narrow[c * 32 : (c + 1) * 32, at] = high
            narrow[64 + c * 32 : 96 + c * 32, at] = low
        return carry

    lax.fori_loop(0, 4, model, 0)

    def back_three(step, carry):
        part = lax.rem(me // 8 + 1 + step, 4)
        rows = pl.ds(pl.multiple_of(part * 256, 256), 256)
        real, imag = back_x(narrow, 64, rows)
        for j in range(8):
            other = part * 8 + j
            three_s[other] = jnp.concatenate(
                [cut(real[0:16], j), cut(imag[0:16], j), cut(real[16:32], j), cut(imag[16:32], j)],
                axis=1,
            )
            to_all(three_s, three_r, 5, other)
        return carry

    lax.fori_loop(0, 4, back_three, 0)
    loads[7].wait()
    loads[8].wait()
    total_of(seen_r, 2).wait_recv()
    total_of(noise_r, 3).wait_recv()
    total_of(three_r, 5).wait_recv()

    def spread_three(source, carry):
        block = three_r[source]
        where = lane_groups(16)
        for c in range(2):
            for h in range(2):
                high, low = split(jnp.where(where == h * 2 + c, block, 0.0))
                rows = pl.ds(pl.multiple_of(source * 64 + c * 32 + h * 16, 16), 16)
                tall[rows, 0:128] = high
                tall[rows, 128:256] = low
        return carry

    lax.fori_loop(0, devices, spread_three, 0)
    normalizer = 1.0 / (size * size)

    def back_y(rows):
        both = mul(gh[rows], tall[...])
        out = both[:, 0:128] + both[:, 128:256] + mul(gl[rows], tall[:, 0:128])
        return out * normalizer

    def residual(step, carry):
        band = lax.rem(my_y + 1 + step, bands)
        rows = pl.ds(pl.multiple_of(band * 256, 256), 256)
        out = fold(back_y(rows))
        blurred = pick_groups([out[g * 64 : (g + 1) * 64] for g in range(num_groups)])
        left_over = noise_r[band] * (blurred - seen_r[band])
        res_s[band] = left_over
        for g in range(num_groups):
            high, low = split(jnp.concatenate([cut(left_over, g)] * num_groups, axis=1))
            rows = pl.ds(pl.multiple_of(band * 256 + g * 64, 64), 64)
            fields[rows, 0:128] = high
            fields[rows, 128:256] = low
        return carry

    lax.fori_loop(0, bands, residual, 0)

    def forward_four(step, carry):
        part, out = along_y(step)
        for j in range(4):
            other = part * 4 + j
            pieces = []
            for h in range(2):
                for c in range(2):
                    row = j * 64 + c * 32 + h * 16
                    pieces.append(out[row : row + 16])
            four_s[other] = pick_groups(pieces)
            to_all(four_s, four_r, 6, other)
        return carry

    lax.fori_loop(0, 8, forward_four, 0)
    for other in range(bands):
        to_band(res_s, res_r, 8, other)
    total_of(four_r, 6).wait_recv()

    def gather_four(g, carry):
        at = pl.ds(pl.multiple_of(g * 128, 128), 128)
        blocks = [four_r[4 * g + j] for j in range(4)]
        for c in range(2):
            for h in range(2):
                high, low = split(
                    jnp.concatenate([cut(block, h * 2 + c) for block in blocks], axis=1)
                )
                row = c * 32 + h * 16
                narrow[row : row + 16, at] = high
                narrow[64 + row : 80 + row, at] = low
        return carry

    lax.fori_loop(0, 8, gather_four, 0)

    def adjoint(step, carry):
        at = pl.ds(pl.multiple_of(step * 256, 256), 256)
        real, imag = along_x(narrow, 64, at)
        for k in range(4):
            trans_real, trans_imag = (trans[k, 0, :, at], trans[k, 1, :, at])
            both = (real * trans_real + imag * trans_imag, imag * trans_real - real * trans_imag)
            for c in range(2):
                high, low = split(both[c])
                row = c * 128 + k * 32
                wide[row : row + 32, at] = high
                wide[256 + row : 288 + row, at] = low
        return carry

    lax.fori_loop(0, 4, adjoint, 0)

    def back_five(step, carry):
        part = lax.rem(me // 8 + 1 + step, 4)
        rows = pl.ds(pl.multiple_of(part * 256, 256), 256)
        both = back_x(wide, 256, rows)
        for j in range(8):
            other = part * 8 + j
            for c in range(2):
                five_s[other, c * 32 : (c + 1) * 32] = jnp.concatenate(
                    [cut(both[c][k * 32 : (k + 1) * 32], j) for k in range(4)], axis=1
                )
            to_all(five_s, five_r, 7, other)
        return carry

    lax.fori_loop(0, 4, back_five, 0)
    total_of(five_r, 7).wait_recv()

    def split_five(source, carry):
        high, low = split(five_r[source])
        rows = pl.ds(pl.multiple_of(source * 64, 64), 64)
        tall[rows, 0:128] = high
        tall[rows, 128:256] = low
        return carry

    lax.fori_loop(0, devices, split_five, 0)

    def finish(step, carry):
        band = lax.rem(my_y + 1 + step, bands)
        rows = pl.ds(pl.multiple_of(band * 256, 256), 256)
        out = fold(back_y(rows) * weights[rows])
        grad_s[band] = pick_groups([out[g * 64 : (g + 1) * 64] for g in range(num_groups)])
        to_band(grad_s, grad_r, 15, band)
        return carry

    lax.fori_loop(0, bands, finish, 0)
    total_of(res_r, 8).wait_recv()
    total_of(grad_r, 15).wait_recv()
    for g in range(num_groups):
        rows = slice(g * 64, (g + 1) * 64)
        res_out[rows] = jnp.concatenate([cut(res_r[band], g) for band in range(bands)], axis=1)
        grad_out[rows] = (
            jnp.concatenate([cut(grad_r[band], g) for band in range(bands)], axis=1)
            - tv_weight * spread[rows]
        )
    for buffer, phase in (
        (sky_s, 0), (tile_s, 1), (seen_s, 2), (noise_s, 3), (two_s, 4), (three_s, 5),
        (four_s, 6), (five_s, 7), (res_s, 8), (grad_s, 15),
    ):
        total_of(buffer, phase).wait_send()


def on_device(sky_image, observed, noise_weight, basis_tiles, intersection, counts, transfer):
    pool, tile_side = (basis_tiles.shape[0], basis_tiles.shape[1])
    shape = (lax.axis_size("sy"), lax.axis_size("sx"), *sky_image.shape, pool, tile_side)
    if shape + intersection.shape[2:] != (bands, band_size, 256, lanes, 4, lanes, 4):
        return generic_device(
            sky_image, observed, noise_weight, basis_tiles, intersection, counts, transfer
        )
    my_band, my_column = (lax.axis_index("sy"), lax.axis_index("sx"))
    lists = intersection.reshape(bands, 2, band_size, 4).transpose(0, 2, 1, 3)
    lists = lists.reshape(bands, band_size, 8)
    slots = jnp.arange(2, dtype=jnp.int32)
    asked = lax.dynamic_index_in_dim(lists, my_band, 0, False)
    local = asked - (my_band * band_size + my_column) * pool
    hit = (local >= 0) & (local < pool)
    earlier = np.tril(np.ones((8, 8), bool), -1)
    rank = jnp.sum((hit[:, None, :] & earlier).astype(jnp.int32), axis=2)
    chosen = (
        hit[:, :, None, None]
        & (local[:, :, None, None] == jnp.arange(pool, dtype=jnp.int32)[:, None])
        & (rank[:, :, None, None] == slots)
    ).any(axis=1)
    tile_mult = jnp.broadcast_to(
        chosen.astype(jnp.float32)[:, :, None, :, None], (band_size, pool, 2, 2, group)
    ).reshape(band_size, pool, lanes)
    wanted = lax.dynamic_index_in_dim(lists, my_column, 1, False)
    holder = wanted // pool - jnp.arange(bands, dtype=jnp.int32)[:, None] * band_size
    same = holder[:, :, None] == holder[:, None, :]
    place = jnp.sum((same & earlier).astype(jnp.int32), axis=2)
    pick = (holder[:, :, None, None] == jnp.arange(band_size, dtype=jnp.int32)[:, None]) & (
        place[:, :, None, None] == slots
    )
    pick_mult = jnp.broadcast_to(
        pick.astype(jnp.float32)[:, :, :, None, :, None], (bands, 8, band_size, 2, 2, group)
    ).reshape(bands * 8, band_size, lanes)
    in_use = (jnp.arange(4, dtype=jnp.int32) < counts.reshape(2, 1)).reshape(8, 1)
    mask = jnp.broadcast_to(in_use.astype(jnp.float32), (8, lanes))
    constants = tables()
    f32, bf16 = (jnp.float32, jnp.bfloat16)

    def double(*dims, kind=f32):
        return [pltpu.VMEM(dims, kind)] * 2

    scratch = [
        pltpu.VMEM(transfer.shape, f32),
        *[pltpu.VMEM(table.shape, bf16) for table in constants],
        *double(bands, 72, lanes),
        *double(bands, 64, lanes),
        *double(bands, 64, lanes),
        *double(devices, 64, lanes, kind=bf16),
        *double(devices, 64, lanes),
        *double(devices, 16, lanes),
        *double(devices, 16, lanes),
        *double(devices, 64, lanes),
        *double(bands, 64, lanes),
        *double(bands, 64, lanes),
        *double(64, lanes),
        *double(8, lanes),
        *double(8, lanes),
        pltpu.VMEM((size, lanes), f32),
        pltpu.VMEM((size, 2 * lanes), bf16),
        pltpu.VMEM((512, size), bf16),
        pltpu.VMEM((128, size), bf16),
        pltpu.VMEM((2 * size, 2 * lanes), bf16),
        pltpu.VMEM((256, lanes), f32),
        pltpu.SemaphoreType.DMA((9,)),
        pltpu.SemaphoreType.DMA((16,)),
        pltpu.SemaphoreType.DMA((16,)),
    ]
    in_vmem = pl.BlockSpec(memory_space=pltpu.VMEM)
    outside = pl.BlockSpec(memory_space=pl.ANY)
    return pl.pallas_call(
        kernel,
        out_shape=[jax.ShapeDtypeStruct(sky_image.shape, f32)] * 2,
        in_specs=[in_vmem] * 7 + [outside] * 9,
        out_specs=[in_vmem] * 2,
        scratch_shapes=scratch,
        compiler_params=pltpu.CompilerParams(
            collective_id=0, has_side_effects=True, vmem_limit_bytes=56 * 1024 * 1024
        ),
        cost_estimate=pl.CostEstimate(
            flops=10_000_000_000, bytes_accessed=30_000_000, transcendentals=0
        ),
    )(
        sky_image, observed, noise_weight, mask, basis_tiles, tile_mult, pick_mult,
        transfer, *(jnp.asarray(table) for table in constants),
    )


def solution(mesh):
    placed = (
        P("sy", "sx"),
        P("sy", "sx"),
        P("sy", "sx"),
        P(("sy", "sx"), None, None),
        P(),
        P("sy", "sx"),
        P(None, None, ("sy", "sx"), None),
    )
    return jax.shard_map(
        on_device,
        mesh=mesh,
        in_specs=placed,
        out_specs=(P("sy", "sx"), P("sy", "sx")),
        check_vma=False,
    )
```

profile of v0, /device:TPU:0, one launch (start us, length us, event | category | flops | bytes accessed | tf_op | source)
XLA Modules:
  0.0 126.7 jit_solution(6827531447760999982)
XLA Ops:
  0.6 0.7 dynamic-slice_subtract_fusion
  1.3 0.1 copy.23
  1.4 0.9 convert_reduce_fusion
  2.3 0.2 and_reduce_fusion
  2.6 0.1 copy.25
  2.7 0.1 broadcast_in_dim.7
  2.8 0.7 reshape.194.tile_mult
  3.5 1.0 dynamic-slice_reduce_fusion
  4.5 0.1 fusion.6
  4.6 0.9 convert_reduce_fusion.1
  5.5 0.1 iota_compare_fusion
  5.6 0.1 iota_compare_fusion.1
  5.6 0.1 and_convert_fusion
  5.8 0.3 broadcast_in_dim.8
  6.1 1.1 reshape.195.pick_mult
  7.2 0.7 compare_convert_fusion
  7.9 0.1 reshape.196
  8.0 0.7 broadcast_in_dim.6.mask
  8.7 114.9 %shard_map.167 = (f32[256,128]{1,0:T(8,128)}, f32[256,128]{1,0:T(8,128)}) custom-call(f32[256,128]{1,0:T(8,128)} %sky.1, f32[256,128]{1,0:T(8,128)} %seen.1, f32[256,128]{1,0:T(8,128)} %noise.1, f32[8,128]{1,0:T(8,128)} %broadcast_in_dim.6.mask, bf16[4,128,128]{2,1,0:T(8,128)(2,1)} %basis.1, f32[8,4,128]{2,1,0:T(4,128)} %reshape.194.tile_mult, ...), custom_call_target="tpu_custom_call" | custom-call | flops 10000000000 | bytes 30000000 | tf_op jit(solution)/shard_map/pallas_call | solution.py:729
  123.6 1.6 %copy.29 = f32[256,128]{1,0:T(8,128)} copy(f32[256,128]{1,0:T(8,128)} %get-tuple-element.6) | data formatting | bytes 262144
  125.2 1.6 %copy.30 = f32[256,128]{1,0:T(8,128)} copy(f32[256,128]{1,0:T(8,128)} %get-tuple-element.7) | data formatting | bytes 262144
  (5 shorter events, 0.0 us)
where the time goes:
time: 129 us; the launch traced here: 127 us
  Pallas kernels  115 us (89%)
  local copies, waits for them, and re-layouts  6.32 us (5%)
  other arithmetic  4.79 us (4%)
    pallas_call x1, Pallas kernels, on_device(): pl.pallas_call(kernel, out_shape=[jax.ShapeDtypeStruct(sky_image.shape, f...  115 us
    unnamed x2, local copies, waits for them, and re-layouts  3.14 us

commit v1 on v0

--- a/solution.py
+++ b/solution.py
@@ -245,6 +245,22 @@
     return values + pltpu.roll(values, 32, 1)
 
 
+def encode(real, imag):
+    largest = jnp.max(jnp.maximum(jnp.abs(real), jnp.abs(imag)), axis=0, keepdims=True)
+    level = jnp.ceil(jnp.log2(jnp.maximum(largest, 1e-30)) * 256.0 + 0.01)
+    factor = 32760.0 * jnp.exp2(level * (-1.0 / 256.0))
+    high = jnp.floor(real * factor + 0.5).astype(jnp.int32)
+    low = jnp.floor(imag * factor + 0.5).astype(jnp.int32)
+    return high * 65536 + (low + 32768), level.astype(jnp.int32)
+
+
+def decode(packed, level):
+    factor = jnp.exp2(level.astype(jnp.float32) * (1.0 / 256.0)) * (1.0 / 32760.0)
+    real = (packed >> 16).astype(jnp.float32) * factor
+    imag = ((packed & 65535) - 32768).astype(jnp.float32) * factor
+    return real, imag
+
+
 def pull(total, sky, left, right, below, above, below_left, above_right):
     rows = sky.shape[0]
     lane = lax.broadcasted_iota(jnp.int32, sky.shape, 1)
@@ -268,7 +284,7 @@
 
 
 def kernel(
-    sky, seen, noise, mask, basis, tile_mult, pick_mult,
+    sky, seen, noise, basis, lists, counts,
     trans_hbm, fyh_hbm, fyl_hbm, cxh_hbm, sxh_hbm, cxl_hbm, sxl_hbm, gh_hbm, gl_hbm,
     res_out, grad_out,
     trans, fyh, fyl, cxh, sxh, cxl, sxl, gh, gl,
@@ -341,9 +357,12 @@
             [cut(block[g * 64 : (g + 1) * 64], other) for g in range(num_groups)], axis=1
         )
 
+    row = lax.broadcasted_iota(jnp.int32, (8, lanes), 0)
+    mask = jnp.where(row % 4 < jnp.where(row < 4, counts[0, 0], counts[1, 0]), 1.0, 0.0)
+    slot_lane = lane_groups(64) % 2
     for other in range(bands):
         sky_s[other, 0:64] = pack(sky[...], other)
-        sky_s[other, 64:72] = mask[...]
+        sky_s[other, 64:72] = mask
     pl.semaphore_wait(barrier, devices - 1)
     for other in range(bands):
         to_band(sky_s, sky_r, 0, other)
@@ -357,9 +376,17 @@
             )
 
         def choose(column, carry):
-            acc = tile_mult[column, 0:1] * packs[0]
+            first, second, seen_before = (-1, -1, 0)
+            for e in range(8):
+                local = lists[my_y * 2 + e // 4, column, e % 4] - me * 4
+                hit = (local >= 0) & (local < 4)
+                first = jnp.where(hit & (seen_before == 0), local, first)
+                second = jnp.where(hit & (seen_before == 1), local, second)
+                seen_before = seen_before + jnp.where(hit, 1, 0)
+            wanted = jnp.where(slot_lane == 0, first, second)
+            acc = jnp.where(wanted == 0, packs[0], 0.0)
             for t in range(1, 4):
-                acc = acc + tile_mult[column, t : t + 1] * packs[t]
+                acc = jnp.where(wanted == t, packs[t], acc)
             tile_s[other * band_size + column] = acc.astype(jnp.bfloat16)
             to_all(tile_s, tile_r, 1, other * band_size + column)
             return carry
@@ -390,13 +417,18 @@
 
     def weigh(band, carry):
         parts = []
+        tiles = [tile_r[band * band_size + h].astype(jnp.float32) for h in range(band_size)]
+        holders = [
+            lists[band * 2 + e // 4, my_x, e % 4] // 4 - band * band_size for e in range(8)
+        ]
         for e in range(8):
-            acc = None
+            slot = 0
+            for earlier in range(e):
+                slot = slot + jnp.where(holders[earlier] == holders[e], 1, 0)
+            place = holders[e] * 2 + slot
+            acc = jnp.zeros((64, lanes), jnp.float32)
             for h in range(band_size):
-                term = pick_mult[band * 8 + e, h : h + 1] * tile_r[band * band_size + h].astype(
-                    jnp.float32
-                )
-                acc = term if acc is None else acc + term
+                acc = jnp.where(slot_lane + 2 * h == place, tiles[h], acc)
             acc = (acc + pltpu.roll(acc, 96, 1)) * sky_r[band, 64 + e : 65 + e]
             parts.append(acc)
         for g in range(num_groups):
@@ -427,7 +459,9 @@
         part, out = along_y(step)
         for j in range(4):
             other = part * 4 + j
-            two_s[other] = out[j * 64 : (j + 1) * 64]
+            packed, level = encode(out[j * 64 : j * 64 + 32], out[j * 64 + 32 : j * 64 + 64])
+            two_s[other, 0:32] = packed
+            two_s[other, 32:40] = jnp.broadcast_to(level, (8, lanes))
             to_all(two_s, two_r, 4, other)
         return carry
 
@@ -459,8 +493,9 @@
 
     def gather_two(g, carry):
         at = pl.ds(pl.multiple_of(g * 128, 128), 128)
+        parts = [decode(two_r[4 * g + j, 0:32], two_r[4 * g + j, 32:33]) for j in range(4)]
         for c in range(2):
-            blocks = [two_r[4 * g + j, c * 32 : (c + 1) * 32] for j in range(4)]
+            blocks = [part[c] for part in parts]
             for k in range(4):
                 high, low = split(jnp.concatenate([cut(block, k) for block in blocks], axis=1))
                 row = c * 128 + k * 32
@@ -612,10 +647,13 @@
         both = back_x(wide, 256, rows)
         for j in range(8):
             other = part * 8 + j
-            for c in range(2):
-                five_s[other, c * 32 : (c + 1) * 32] = jnp.concatenate(
-                    [cut(both[c][k * 32 : (k + 1) * 32], j) for k in range(4)], axis=1
-                )
+            real, imag = [
+                jnp.concatenate([cut(part[k * 32 : (k + 1) * 32], j) for k in range(4)], axis=1)
+                for part in both
+            ]
+            packed, level = encode(real, imag)
+            five_s[other, 0:32] = packed
+            five_s[other, 32:40] = jnp.broadcast_to(level, (8, lanes))
             to_all(five_s, five_r, 7, other)
         return carry
 
@@ -623,10 +661,12 @@
     total_of(five_r, 7).wait_recv()
 
     def split_five(source, carry):
-        high, low = split(five_r[source])
-        rows = pl.ds(pl.multiple_of(source * 64, 64), 64)
-        tall[rows, 0:128] = high
-        tall[rows, 128:256] = low
+        parts = decode(five_r[source, 0:32], five_r[source, 32:33])
+        for c in range(2):
+            high, low = split(parts[c])
+            rows = pl.ds(pl.multiple_of(source * 64 + c * 32, 32), 32)
+            tall[rows, 0:128] = high
+            tall[rows, 128:256] = low
         return carry
 
     lax.fori_loop(0, devices, split_five, 0)
@@ -663,37 +703,9 @@
         return generic_device(
             sky_image, observed, noise_weight, basis_tiles, intersection, counts, transfer
         )
-    my_band, my_column = (lax.axis_index("sy"), lax.axis_index("sx"))
-    lists = intersection.reshape(bands, 2, band_size, 4).transpose(0, 2, 1, 3)
-    lists = lists.reshape(bands, band_size, 8)
-    slots = jnp.arange(2, dtype=jnp.int32)
-    asked = lax.dynamic_index_in_dim(lists, my_band, 0, False)
-    local = asked - (my_band * band_size + my_column) * pool
-    hit = (local >= 0) & (local < pool)
-    earlier = np.tril(np.ones((8, 8), bool), -1)
-    rank = jnp.sum((hit[:, None, :] & earlier).astype(jnp.int32), axis=2)
-    chosen = (
-        hit[:, :, None, None]
-        & (local[:, :, None, None] == jnp.arange(pool, dtype=jnp.int32)[:, None])
-        & (rank[:, :, None, None] == slots)
-    ).any(axis=1)
-    tile_mult = jnp.broadcast_to(
-        chosen.astype(jnp.float32)[:, :, None, :, None], (band_size, pool, 2, 2, group)
-    ).reshape(band_size, pool, lanes)
-    wanted = lax.dynamic_index_in_dim(lists, my_column, 1, False)
-    holder = wanted // pool - jnp.arange(bands, dtype=jnp.int32)[:, None] * band_size
-    same = holder[:, :, None] == holder[:, None, :]
-    place = jnp.sum((same & earlier).astype(jnp.int32), axis=2)
-    pick = (holder[:, :, None, None] == jnp.arange(band_size, dtype=jnp.int32)[:, None]) & (
-        place[:, :, None, None] == slots
-    )
-    pick_mult = jnp.broadcast_to(
-        pick.astype(jnp.float32)[:, :, :, None, :, None], (bands, 8, band_size, 2, 2, group)
-    ).reshape(bands * 8, band_size, lanes)
-    in_use = (jnp.arange(4, dtype=jnp.int32) < counts.reshape(2, 1)).reshape(8, 1)
-    mask = jnp.broadcast_to(in_use.astype(jnp.float32), (8, lanes))
     constants = tables()
     f32, bf16 = (jnp.float32, jnp.bfloat16)
+    scalars = pl.BlockSpec(memory_space=pltpu.SMEM)
 
     def double(*dims, kind=f32):
         return [pltpu.VMEM(dims, kind)] * 2
@@ -705,10 +717,10 @@
         *double(bands, 64, lanes),
         *double(bands, 64, lanes),
         *double(devices, 64, lanes, kind=bf16),
-        *double(devices, 64, lanes),
+        *double(devices, 40, lanes, kind=jnp.int32),
         *double(devices, 16, lanes),
         *double(devices, 16, lanes),
-        *double(devices, 64, lanes),
+        *double(devices, 40, lanes, kind=jnp.int32),
         *double(bands, 64, lanes),
         *double(bands, 64, lanes),
         *double(64, lanes),
@@ -729,7 +741,7 @@
     return pl.pallas_call(
         kernel,
         out_shape=[jax.ShapeDtypeStruct(sky_image.shape, f32)] * 2,
-        in_specs=[in_vmem] * 7 + [outside] * 9,
+        in_specs=[in_vmem] * 4 + [scalars] * 2 + [outside] * 9,
         out_specs=[in_vmem] * 2,
         scratch_shapes=scratch,
         compiler_params=pltpu.CompilerParams(
@@ -739,8 +751,7 @@
             flops=10_000_000_000, bytes_accessed=30_000_000, transcendentals=0
         ),
     )(
-        sky_image, observed, noise_weight, mask, basis_tiles, tile_mult, pick_mult,
-        transfer, *(jnp.asarray(table) for table in constants),
+        sky_image, observed, noise_weight, basis_tiles, intersection, counts, transfer, *(jnp.asarray(table) for table in constants),
     )
 
 

time: 129 us -> 108 us (0.84); the launches traced: 127 us -> 107 us
  Pallas kernels: 115 us -> 101 us
  other arithmetic: 4.79 us -> 0 us
    pallas_call x1, Pallas kernels: 115 us -> 101 us  [on_device(): pl.pallas_call(kernel, out_shape=[jax.ShapeDtypeStruct(sky_image.shape, f...]
    unnamed x2 -> x4, local copies, waits for them, and re-layouts: 3.14 us -> 5.88 us
    reshape x2 -> x0, local copies, waits for them, and re-layouts: 1.82 us -> none  [the longest x1 1.1 us: on_device(): pick_mult = jnp.broadcast_to(pick.astype(jnp.float32)[:, :, :, None, :, N...]
    reduce_sum x2 -> x0, other arithmetic: 1.78 us -> none  [the longest x1 0.89 us: on_device(): rank = jnp.sum((hit[:, None, :] & earlier).astype(jnp.int32), axis=2)]
where the time goes in v1:
time: 108 us; the launch traced here: 107 us
  Pallas kernels  101 us (94%)
  local copies, waits for them, and re-layouts  5.88 us (5%)
    pallas_call x1, Pallas kernels, on_device(): pl.pallas_call(kernel, out_shape=[jax.ShapeDtypeStruct(sky_image.shape, f...  101 us
    unnamed x4, local copies, waits for them, and re-layouts  5.88 us

profile of v1, /device:TPU:0, one launch (start us, length us, event | category | flops | bytes accessed | tf_op | source)
XLA Modules:
  0.0 107.3 jit_solution(2257274233911316497)
XLA Ops:
  0.6 1.3 %copy.18.counts = s32[2,1]{1,0:T(2,128)} copy(s32[2,1]{0,1:T(1,128)} %param.20) | data formatting | bytes 16 | tf_op args[5]
  1.9 1.4 %copy.17.lists = s32[8,8,4]{2,1,0:T(8,128)} copy(s32[8,8,4]{1,2,0:T(4,128)} %param.19) | data formatting | bytes 2048 | tf_op args[4]
  3.4 100.8 %shard_map.158 = (f32[256,128]{1,0:T(8,128)}, f32[256,128]{1,0:T(8,128)}) custom-call(f32[256,128]{1,0:T(8,128)} %sky.1, f32[256,128]{1,0:T(8,128)} %seen.1, f32[256,128]{1,0:T(8,128)} %noise.1, bf16[4,128,128]{2,1,0:T(8,128)(2,1)} %basis.1, s32[8,8,4]{2,1,0:T(8,128)} %copy.17.lists, s32[2,1]{1,0:T(2,128)} %copy.18.counts, f32[4,2,32,1024]{3,2,1,0:T(8,128)} %trans_hbm.1, ...), custom_call_target="tpu_custom_call" | custom-call | flops 10000000000 | bytes 30000000 | tf_op jit(solution)/shard_map/pallas_call | solution.py:741
  104.2 1.6 %copy.21 = f32[256,128]{1,0:T(8,128)} copy(f32[256,128]{1,0:T(8,128)} %get-tuple-element.4) | data formatting | bytes 262144
  105.8 1.6 %copy.22 = f32[256,128]{1,0:T(8,128)} copy(f32[256,128]{1,0:T(8,128)} %get-tuple-element.5) | data formatting | bytes 262144

commit v2 on v1

--- a/solution.py
+++ b/solution.py
@@ -292,7 +292,7 @@
     two_s, two_r, three_s, three_r, four_s, four_r, five_s, five_r,
     res_s, res_r, grad_s, grad_r,
     halo_left, halo_right, halo_below, halo_above, halo_bl, halo_ar,
-    weights, fields, wide, narrow, tall, spread,
+    weights, fields, wide, narrow, tall, spread, spectra, pulled,
     load_sem, send_sem, recv_sem,
 ):
     my_y, my_x = (lax.axis_index("sy"), lax.axis_index("sx"))
@@ -317,26 +317,36 @@
         loads.append(pltpu.make_async_copy(source, target, load_sem.at[index]))
         loads[-1].start()
 
-    def send(source, target, phase, where):
+    def send(source, target, phase, where, arrival=None):
+        arrival = phase if arrival is None else arrival
         pltpu.make_async_remote_copy(
             src_ref=source, dst_ref=target, send_sem=send_sem.at[phase],
-            recv_sem=recv_sem.at[phase], device_id=where, device_id_type=MESH,
+            recv_sem=recv_sem.at[arrival], device_id=where, device_id_type=MESH,
         ).start()
 
-    def total_of(buffer, phase):
-        part = buffer.at[pl.ds(0, buffer.shape[0] - 1)]
+    def total_of(buffer, phase, count=None):
+        part = buffer.at[pl.ds(0, buffer.shape[0] - 1 if count is None else count)]
         return pltpu.make_async_remote_copy(
             src_ref=part, dst_ref=part, send_sem=send_sem.at[phase],
             recv_sem=recv_sem.at[phase], device_id=(lax.rem(my_y + 1, bands), my_x),
             device_id_type=MESH,
         )
 
-    def to_all(source, target, phase, other):
+    def arrived(buffer, first, plane):
+        @pl.when(plane != my_y)
+        def _():
+            total_of(buffer, first + plane, band_size).wait_recv()
+
+        @pl.when(plane == my_y)
+        def _():
+            total_of(buffer, first + plane, band_size - 1).wait_recv()
+
+    def to_all(source, target, phase, other, arrival=None):
         @pl.when(other != me)
         def _():
             send(
                 source.at[other], target.at[me], phase,
-                (other // band_size, lax.rem(other, band_size)),
+                (other // band_size, lax.rem(other, band_size)), arrival,
             )
 
         @pl.when(other == me)
@@ -364,8 +374,8 @@
         sky_s[other, 0:64] = pack(sky[...], other)
         sky_s[other, 64:72] = mask
     pl.semaphore_wait(barrier, devices - 1)
-    for other in range(bands):
-        to_band(sky_s, sky_r, 0, other)
+    for step in range(bands):
+        to_band(sky_s, sky_r, 0, lax.rem(my_y + 1 + step, bands))
 
     for other in range(bands):
         packs = []
@@ -388,16 +398,23 @@
             for t in range(1, 4):
                 acc = jnp.where(wanted == t, packs[t], acc)
             tile_s[other * band_size + column] = acc.astype(jnp.bfloat16)
-            to_all(tile_s, tile_r, 1, other * band_size + column)
             return carry
 
         lax.fori_loop(0, band_size, choose, 0)
+
+    def send_tiles(step, carry):
+        plane = lax.rem(my_y + 1 + step // band_size, bands)
+        to_all(tile_s, tile_r, 1, plane * band_size + lax.rem(my_x + step, band_size))
+        return carry
+
+    lax.fori_loop(0, devices, send_tiles, 0)
 
     for other in range(bands):
         seen_s[other] = pack(seen[...], other)
         noise_s[other] = pack(noise[...], other)
-        to_band(seen_s, seen_r, 2, other)
-        to_band(noise_s, noise_r, 3, other)
+    for step in range(bands):
+        to_band(seen_s, seen_r, 2, lax.rem(my_y + 1 + step, bands))
+        to_band(noise_s, noise_r, 3, lax.rem(my_y + 1 + step, bands))
     up, down = (lax.rem(my_y + bands - 1, bands), lax.rem(my_y + 1, bands))
     west, east = (lax.rem(my_x + band_size - 1, band_size), lax.rem(my_x + 1, band_size))
     first, last = (sky.at[pl.ds(0, 8)], sky.at[pl.ds(248, 8)])
@@ -450,7 +467,7 @@
     loads[1].wait()
 
     def along_y(step):
-        part = lax.rem(me // 4 + 1 + step, 8)
+        part = lax.rem(my_y + 1 + step // 2, bands) * 2 + lax.rem(step + my_x, 2)
         rows = pl.ds(pl.multiple_of(part * 256, 256), 256)
         both = mul(fyh[rows], fields[...])
         return part, both[:, 0:128] + both[:, 128:256] + mul(fyl[rows], fields[:, 0:128])
@@ -462,7 +479,8 @@
             packed, level = encode(out[j * 64 : j * 64 + 32], out[j * 64 + 32 : j * 64 + 64])
             two_s[other, 0:32] = packed
             two_s[other, 32:40] = jnp.broadcast_to(level, (8, lanes))
-            to_all(two_s, two_r, 4, other)
+        for j in range(4):
+            to_all(two_s, two_r, 4, part * 4 + lax.rem(my_x + j, 4), 16 + my_y)
         return carry
 
     lax.fori_loop(0, 8, forward_y, 0)
@@ -489,9 +507,8 @@
 
     for index in range(2, 7):
         loads[index].wait()
-    total_of(two_r, 4).wait_recv()
-
-    def gather_two(g, carry):
+
+    def gather_two(g):
         at = pl.ds(pl.multiple_of(g * 128, 128), 128)
         parts = [decode(two_r[4 * g + j, 0:32], two_r[4 * g + j, 32:33]) for j in range(4)]
         for c in range(2):
@@ -501,17 +518,31 @@
                 row = c * 128 + k * 32
                 wide[row : row + 32, at] = high
                 wide[256 + row : 288 + row, at] = low
-        return carry
-
-    lax.fori_loop(0, 8, gather_two, 0)
-
-    def along_x(buffer, half, at):
-        cos_part = mul(buffer[...], cxh[:, at])
-        sin_part = mul(buffer[...], sxh[:, at])
-        cos_part = cos_part[0:half] + cos_part[half:] + mul(buffer[0:half], cxl[:, at])
-        sin_part = sin_part[0:half] + sin_part[half:] + mul(buffer[0:half], sxl[:, at])
+
+    def along_x(buffer, half, at, inner):
+        cos_part = mul(buffer[:, inner], cxh[inner, at])
+        sin_part = mul(buffer[:, inner], sxh[inner, at])
+        cos_part = cos_part[0:half] + cos_part[half:] + mul(buffer[0:half, inner], cxl[inner, at])
+        sin_part = sin_part[0:half] + sin_part[half:] + mul(buffer[0:half, inner], sxl[inner, at])
         q = half // 2
         return cos_part[0:q] + sin_part[q:half], cos_part[q:half] - sin_part[0:q]
+
+    spectra[...] = jnp.zeros_like(spectra)
+
+    def add_plane(step, carry):
+        plane = lax.rem(my_y + bands - 1 - step, bands)
+        arrived(two_r, 16, plane)
+        gather_two(plane * 2)
+        gather_two(plane * 2 + 1)
+        inner = pl.ds(pl.multiple_of(plane * 256, 256), 256)
+        for n in range(4):
+            at = slice(n * 256, (n + 1) * 256)
+            real, imag = along_x(wide, 256, at, inner)
+            spectra[0, :, at] += real
+            spectra[1, :, at] += imag
+        return carry
+
+    lax.fori_loop(0, bands, add_plane, 0)
 
     def back_x(buffer, half, rows):
         cos_part = mul_t(buffer[...], cxh[rows])
@@ -523,7 +554,7 @@
 
     def model(step, carry):
         at = pl.ds(pl.multiple_of(step * 256, 256), 256)
-        real, imag = along_x(wide, 256, at)
+        real, imag = (spectra[0, :, at], spectra[1, :, at])
         sum_real, sum_imag = (0.0, 0.0)
         for k in range(4):
             rows = slice(k * 32, (k + 1) * 32)
@@ -548,7 +579,8 @@
                 [cut(real[0:16], j), cut(imag[0:16], j), cut(real[16:32], j), cut(imag[16:32], j)],
                 axis=1,
             )
-            to_all(three_s, three_r, 5, other)
+        for j in range(8):
+            to_all(three_s, three_r, 5, part * 8 + lax.rem(my_x + j, 8))
         return carry
 
     lax.fori_loop(0, 4, back_three, 0)
@@ -603,7 +635,8 @@
                     row = j * 64 + c * 32 + h * 16
                     pieces.append(out[row : row + 16])
             four_s[other] = pick_groups(pieces)
-            to_all(four_s, four_r, 6, other)
+        for j in range(4):
+            to_all(four_s, four_r, 6, part * 4 + lax.rem(my_x + j, 4))
         return carry
 
     lax.fori_loop(0, 8, forward_four, 0)
@@ -628,7 +661,7 @@
 
     def adjoint(step, carry):
         at = pl.ds(pl.multiple_of(step * 256, 256), 256)
-        real, imag = along_x(narrow, 64, at)
+        real, imag = along_x(narrow, 64, at, slice(None))
         for k in range(4):
             trans_real, trans_imag = (trans[k, 0, :, at], trans[k, 1, :, at])
             both = (real * trans_real + imag * trans_imag, imag * trans_real - real * trans_imag)
@@ -654,11 +687,12 @@
             packed, level = encode(real, imag)
             five_s[other, 0:32] = packed
             five_s[other, 32:40] = jnp.broadcast_to(level, (8, lanes))
-            to_all(five_s, five_r, 7, other)
+        for j in range(8):
+            to_all(five_s, five_r, 7, part * 8 + lax.rem(my_x + j, 8), 20 + my_y)
         return carry
 
     lax.fori_loop(0, 4, back_five, 0)
-    total_of(five_r, 7).wait_recv()
+    pulled[...] = jnp.zeros_like(pulled)
 
     def split_five(source, carry):
         parts = decode(five_r[source, 0:32], five_r[source, 32:33])
@@ -669,12 +703,24 @@
             tall[rows, 128:256] = low
         return carry
 
-    lax.fori_loop(0, devices, split_five, 0)
+    def add_five(step, carry):
+        plane = lax.rem(my_y + bands - 1 - step, bands)
+        arrived(five_r, 20, plane)
+        lax.fori_loop(plane * band_size, (plane + 1) * band_size, split_five, 0)
+        inner = pl.ds(pl.multiple_of(plane * 512, 512), 512)
+        for band in range(bands):
+            rows = slice(band * 256, (band + 1) * 256)
+            both = mul(gh[rows, inner], tall[inner])
+            both = both[:, 0:128] + both[:, 128:256] + mul(gl[rows, inner], tall[inner, 0:128])
+            pulled[rows] += both
+        return carry
+
+    lax.fori_loop(0, bands, add_five, 0)
 
     def finish(step, carry):
         band = lax.rem(my_y + 1 + step, bands)
         rows = pl.ds(pl.multiple_of(band * 256, 256), 256)
-        out = fold(back_y(rows) * weights[rows])
+        out = fold(pulled[rows] * weights[rows] * normalizer)
         grad_s[band] = pick_groups([out[g * 64 : (g + 1) * 64] for g in range(num_groups)])
         to_band(grad_s, grad_r, 15, band)
         return carry
@@ -732,9 +778,11 @@
         pltpu.VMEM((128, size), bf16),
         pltpu.VMEM((2 * size, 2 * lanes), bf16),
         pltpu.VMEM((256, lanes), f32),
+        pltpu.VMEM((2, lanes, size), f32),
+        pltpu.VMEM((size, lanes), f32),
         pltpu.SemaphoreType.DMA((9,)),
         pltpu.SemaphoreType.DMA((16,)),
-        pltpu.SemaphoreType.DMA((16,)),
+        pltpu.SemaphoreType.DMA((24,)),
     ]
     in_vmem = pl.BlockSpec(memory_space=pltpu.VMEM)
     outside = pl.BlockSpec(memory_space=pl.ANY)

time: 108 us -> 108 us (level)
  no operation moved by 1% of the time
where the time goes in v2:
time: 108 us
  Pallas kernels  101 us (94%)
  local copies, waits for them, and re-layouts  5.88 us (5%)
    pallas_call x1, Pallas kernels, on_device(): pl.pallas_call(kernel, out_shape=[jax.ShapeDtypeStruct(sky_image.shape, f...  101 us
    unnamed x4, local copies, waits for them, and re-layouts  5.88 us

profile of v2, /device:TPU:0, one launch (start us, length us, event | category | flops | bytes accessed | tf_op | source)
XLA Modules:
  0.0 108.0 jit_solution(1532824577737184428)
XLA Ops:
  0.6 1.3 %copy.18.counts = s32[2,1]{1,0:T(2,128)} copy(s32[2,1]{0,1:T(1,128)} %param.20) | data formatting | bytes 16 | tf_op args[5]
  1.9 1.4 %copy.17.lists = s32[8,8,4]{2,1,0:T(8,128)} copy(s32[8,8,4]{1,2,0:T(4,128)} %param.19) | data formatting | bytes 2048 | tf_op args[4]
  3.4 101.5 %shard_map.158 = (f32[256,128]{1,0:T(8,128)}, f32[256,128]{1,0:T(8,128)}) custom-call(f32[256,128]{1,0:T(8,128)} %sky.1, f32[256,128]{1,0:T(8,128)} %seen.1, f32[256,128]{1,0:T(8,128)} %noise.1, bf16[4,128,128]{2,1,0:T(8,128)(2,1)} %basis.1, s32[8,8,4]{2,1,0:T(8,128)} %copy.17.lists, s32[2,1]{1,0:T(2,128)} %copy.18.counts, f32[4,2,32,1024]{3,2,1,0:T(8,128)} %trans_hbm.1, ...), custom_call_target="tpu_custom_call" | custom-call | flops 10000000000 | bytes 30000000 | tf_op jit(solution)/shard_map/pallas_call | solution.py:789
  104.8 1.6 %copy.21 = f32[256,128]{1,0:T(8,128)} copy(f32[256,128]{1,0:T(8,128)} %get-tuple-element.4) | data formatting | bytes 262144
  106.4 1.6 %copy.22 = f32[256,128]{1,0:T(8,128)} copy(f32[256,128]{1,0:T(8,128)} %get-tuple-element.5) | data formatting | bytes 262144

commit v3 on v2

--- a/solution.py
+++ b/solution.py
@@ -206,6 +206,7 @@
         cos_low,
         sin_low,
         *split_table(np.ascontiguousarray(along_y.T)),
+        *(np.ascontiguousarray(part.T) for part in (cos_high, sin_high, cos_low, sin_low)),
     )
 
 
@@ -216,12 +217,6 @@
 
 def mul(left, right):
     return jnp.dot(left, right, preferred_element_type=jnp.float32)
-
-
-def mul_t(left, right):
-    return lax.dot_general(
-        left, right, (((1,), (1,)), ((), ())), preferred_element_type=jnp.float32
-    )
 
 
 def cut(values, index):
@@ -286,8 +281,9 @@
 def kernel(
     sky, seen, noise, basis, lists, counts,
     trans_hbm, fyh_hbm, fyl_hbm, cxh_hbm, sxh_hbm, cxl_hbm, sxl_hbm, gh_hbm, gl_hbm,
+    txh_hbm, uxh_hbm, txl_hbm, uxl_hbm,
     res_out, grad_out,
-    trans, fyh, fyl, cxh, sxh, cxl, sxl, gh, gl,
+    trans, fyh, fyl, cxh, sxh, cxl, sxl, gh, gl, txh, uxh, txl, uxl,
     sky_s, sky_r, seen_s, seen_r, noise_s, noise_r, tile_s, tile_r,
     two_s, two_r, three_s, three_r, four_s, four_r, five_s, five_r,
     res_s, res_r, grad_s, grad_r,
@@ -299,6 +295,9 @@
     me = my_y * band_size + my_x
     barrier = pltpu.get_barrier_semaphore()
 
+    def plane_at(step):
+        return lax.rem(my_y // 2 + step // 2, 2) * 2 + lax.rem(my_y + step, 2)
+
     def greet(step, carry):
         other = lax.rem(me + step, devices)
         pl.semaphore_signal(
@@ -311,7 +310,8 @@
     loads = []
     pairs = (
         (fyh_hbm, fyh), (fyl_hbm, fyl), (cxh_hbm, cxh), (sxh_hbm, sxh), (cxl_hbm, cxl),
-        (sxl_hbm, sxl), (trans_hbm, trans), (gh_hbm, gh), (gl_hbm, gl),
+        (sxl_hbm, sxl), (trans_hbm, trans), (txh_hbm, txh), (uxh_hbm, uxh), (txl_hbm, txl),
+        (uxl_hbm, uxl), (gh_hbm, gh), (gl_hbm, gl),
     )
     for index, (source, target) in enumerate(pairs):
         loads.append(pltpu.make_async_copy(source, target, load_sem.at[index]))
@@ -403,7 +403,7 @@
         lax.fori_loop(0, band_size, choose, 0)
 
     def send_tiles(step, carry):
-        plane = lax.rem(my_y + 1 + step // band_size, bands)
+        plane = plane_at(3 - step // band_size)
         to_all(tile_s, tile_r, 1, plane * band_size + lax.rem(my_x + step, band_size))
         return carry
 
@@ -467,7 +467,7 @@
     loads[1].wait()
 
     def along_y(step):
-        part = lax.rem(my_y + 1 + step // 2, bands) * 2 + lax.rem(step + my_x, 2)
+        part = plane_at(3 - step // 2) * 2 + lax.rem(step + my_x, 2)
         rows = pl.ds(pl.multiple_of(part * 256, 256), 256)
         both = mul(fyh[rows], fields[...])
         return part, both[:, 0:128] + both[:, 128:256] + mul(fyl[rows], fields[:, 0:128])
@@ -530,7 +530,7 @@
     spectra[...] = jnp.zeros_like(spectra)
 
     def add_plane(step, carry):
-        plane = lax.rem(my_y + bands - 1 - step, bands)
+        plane = plane_at(step)
         arrived(two_r, 16, plane)
         gather_two(plane * 2)
         gather_two(plane * 2 + 1)
@@ -545,10 +545,10 @@
     lax.fori_loop(0, bands, add_plane, 0)
 
     def back_x(buffer, half, rows):
-        cos_part = mul_t(buffer[...], cxh[rows])
-        sin_part = mul_t(buffer[...], sxh[rows])
-        cos_part = cos_part[0:half] + cos_part[half:] + mul_t(buffer[0:half], cxl[rows])
-        sin_part = sin_part[0:half] + sin_part[half:] + mul_t(buffer[0:half], sxl[rows])
+        cos_part = mul(buffer[...], txh[:, rows])
+        sin_part = mul(buffer[...], uxh[:, rows])
+        cos_part = cos_part[0:half] + cos_part[half:] + mul(buffer[0:half], txl[:, rows])
+        sin_part = sin_part[0:half] + sin_part[half:] + mul(buffer[0:half], uxl[:, rows])
         q = half // 2
         return cos_part[0:q] - sin_part[q:half], cos_part[q:half] + sin_part[0:q]
 
@@ -569,8 +569,11 @@
 
     lax.fori_loop(0, 4, model, 0)
 
+    for index in range(7, 11):
+        loads[index].wait()
+
     def back_three(step, carry):
-        part = lax.rem(me // 8 + 1 + step, 4)
+        part = plane_at(3 - step)
         rows = pl.ds(pl.multiple_of(part * 256, 256), 256)
         real, imag = back_x(narrow, 64, rows)
         for j in range(8):
@@ -584,8 +587,8 @@
         return carry
 
     lax.fori_loop(0, 4, back_three, 0)
-    loads[7].wait()
-    loads[8].wait()
+    loads[11].wait()
+    loads[12].wait()
     total_of(seen_r, 2).wait_recv()
     total_of(noise_r, 3).wait_recv()
     total_of(three_r, 5).wait_recv()
@@ -610,7 +613,7 @@
         return out * normalizer
 
     def residual(step, carry):
-        band = lax.rem(my_y + 1 + step, bands)
+        band = plane_at(3 - step)
         rows = pl.ds(pl.multiple_of(band * 256, 256), 256)
         out = fold(back_y(rows))
         blurred = pick_groups([out[g * 64 : (g + 1) * 64] for g in range(num_groups)])
@@ -675,7 +678,7 @@
     lax.fori_loop(0, 4, adjoint, 0)
 
     def back_five(step, carry):
-        part = lax.rem(me // 8 + 1 + step, 4)
+        part = plane_at(3 - step)
         rows = pl.ds(pl.multiple_of(part * 256, 256), 256)
         both = back_x(wide, 256, rows)
         for j in range(8):
@@ -704,7 +707,7 @@
         return carry
 
     def add_five(step, carry):
-        plane = lax.rem(my_y + bands - 1 - step, bands)
+        plane = plane_at(step)
         arrived(five_r, 20, plane)
         lax.fori_loop(plane * band_size, (plane + 1) * band_size, split_five, 0)
         inner = pl.ds(pl.multiple_of(plane * 512, 512), 512)
@@ -718,7 +721,7 @@
     lax.fori_loop(0, bands, add_five, 0)
 
     def finish(step, carry):
-        band = lax.rem(my_y + 1 + step, bands)
+        band = plane_at(3 - step)
         rows = pl.ds(pl.multiple_of(band * 256, 256), 256)
         out = fold(pulled[rows] * weights[rows] * normalizer)
         grad_s[band] = pick_groups([out[g * 64 : (g + 1) * 64] for g in range(num_groups)])
@@ -780,7 +783,7 @@
         pltpu.VMEM((256, lanes), f32),
         pltpu.VMEM((2, lanes, size), f32),
         pltpu.VMEM((size, lanes), f32),
-        pltpu.SemaphoreType.DMA((9,)),
+        pltpu.SemaphoreType.DMA((13,)),
         pltpu.SemaphoreType.DMA((16,)),
         pltpu.SemaphoreType.DMA((24,)),
     ]
@@ -789,7 +792,7 @@
     return pl.pallas_call(
         kernel,
         out_shape=[jax.ShapeDtypeStruct(sky_image.shape, f32)] * 2,
-        in_specs=[in_vmem] * 4 + [scalars] * 2 + [outside] * 9,
+        in_specs=[in_vmem] * 4 + [scalars] * 2 + [outside] * 13,
         out_specs=[in_vmem] * 2,
         scratch_shapes=scratch,
         compiler_params=pltpu.CompilerParams(

time: 108 us -> 103 us (0.954)
  Pallas kernels: 101 us -> 96.6 us
    pallas_call x1, Pallas kernels: 101 us -> 96.6 us  [on_device(): pl.pallas_call(kernel, out_shape=[jax.ShapeDtypeStruct(sky_image.shape, f...]
where the time goes in v3:
time: 103 us
  Pallas kernels  96.6 us (94%)
  local copies, waits for them, and re-layouts  5.88 us (6%)
    pallas_call x1, Pallas kernels, on_device(): pl.pallas_call(kernel, out_shape=[jax.ShapeDtypeStruct(sky_image.shape, f...  96.6 us
    unnamed x4, local copies, waits for them, and re-layouts  5.88 us

profile of v3, /device:TPU:0, one launch (start us, length us, event | category | flops | bytes accessed | tf_op | source)
XLA Modules:
  0.0 103.2 jit_solution(7547449847312349828)
XLA Ops:
  0.6 1.3 %copy.22.counts = s32[2,1]{1,0:T(2,128)} copy(s32[2,1]{0,1:T(1,128)} %param.24) | data formatting | bytes 16 | tf_op args[5]
  1.9 1.4 %copy.21.lists = s32[8,8,4]{2,1,0:T(8,128)} copy(s32[8,8,4]{1,2,0:T(4,128)} %param.23) | data formatting | bytes 2048 | tf_op args[4]
  3.4 96.6 %shard_map.194 = (f32[256,128]{1,0:T(8,128)}, f32[256,128]{1,0:T(8,128)}) custom-call(f32[256,128]{1,0:T(8,128)} %sky.1, f32[256,128]{1,0:T(8,128)} %seen.1, f32[256,128]{1,0:T(8,128)} %noise.1, bf16[4,128,128]{2,1,0:T(8,128)(2,1)} %basis.1, s32[8,8,4]{2,1,0:T(8,128)} %copy.21.lists, s32[2,1]{1,0:T(2,128)} %copy.22.counts, f32[4,2,32,1024]{3,2,1,0:T(8,128)} %trans_hbm.1, ...), custom_call_target="tpu_custom_call" | custom-call | flops 10000000000 | bytes 30000000 | tf_op jit(solution)/shard_map/pallas_call | solution.py:792
  100.0 1.6 %copy.25 = f32[256,128]{1,0:T(8,128)} copy(f32[256,128]{1,0:T(8,128)} %get-tuple-element.4) | data formatting | bytes 262144
  101.6 1.6 %copy.26 = f32[256,128]{1,0:T(8,128)} copy(f32[256,128]{1,0:T(8,128)} %get-tuple-element.5) | data formatting | bytes 262144
